TPU v7x, 32 devices: a whole 2x2x4 slice. The times are simulated.
32 devices in a mesh: groups: 2 (over x), stem: 8 (over z, y), cuts: 2 (over core).
Axes of the slice: x: 2, y: 2, z: 4, core: 2. Of those that a mesh axis runs over, the one named last changes fastest.
Arguments:
- stem: bfloat16 [4, 2, 4096, 1024], P(('groups', 'cuts'), None, 'stem'), parts along dimension 0, may hold values from -6 to 6
- edge_values: int32 [4, 4], P(('groups', 'cuts')), parts along dimension 0, may hold values from 0 to 1
- index_order: int32 [1024], replicated, may hold values from 0 to 1023, each once
- branch_first: bfloat16 [2, 1024, 1024], replicated, may hold values from -0.125 to 0.125
- branch_second: bfloat16 [2, 1024, 1024], replicated, may hold values from -0.125 to 0.125
- branch_third: bfloat16 [2, 1024, 256], replicated, may hold values from -0.125 to 0.125
- edge_table: float32 [16, 2, 256], replicated, may hold values from -6 to 6
- picks: int32 [4096], P('stem'), may hold values from 0 to 511, as said below
Outputs:
- amplitudes: float32 [2, 8192, 256], P(None, ('groups', 'stem')), parts along dimension 1
There are 2 independent parts, one for each index of `groups`. A program takes and returns all parts, laid end to end along the dimension named above; an argument that names none is the same for every part. Nothing has to cross between parts.
Inputs may be any that keep to these rules, and one draw needn't show every extreme that they name: `index_order`: each number of 0 to 1023 once. `picks`: each aligned block of 512 entries names every number of 0 to 511 once.
All inputs are finite; a program needn't handle non-finite values.
Results may differ from a plain program's by a relative error of at most 0.0041.
Values may be sent and summed in bfloat16 or wider, within the bound.
A program may use at most 64 MiB of HBM per device.

v0:
```python
import jax
import jax.numpy as jnp
from jax import lax
from jax.sharding import PartitionSpec as P


def swapped(value, axis, distance):
    mask = 2**distance
    pairs = [(source, source ^ mask) for source in range(lax.axis_size(axis))]
    return lax.ppermute(value, axis, pairs)


def complex_dot(operand, matrix):
    real = jnp.dot(operand[0], matrix[0], preferred_element_type=jnp.float32) - jnp.dot(
        operand[1], matrix[1], preferred_element_type=jnp.float32
    )
    imag = jnp.dot(operand[0], matrix[1], preferred_element_type=jnp.float32) + jnp.dot(
        operand[1], matrix[0], preferred_element_type=jnp.float32
    )
    return jnp.stack([real, imag])


def on_device(
    stem, edge_values, index_order, branch_first, branch_second, branch_third, edge_table, picks
):
    stem_size = lax.axis_size("stem")
    bit_pos = stem_size.bit_length() - 2
    top_bit = lax.axis_index("stem") // (stem_size // 2) % 2
    is_low = top_bit == 0
    width = branch_first.shape[1]
    half_width = width // 2
    rows_dev = stem.shape[2]
    block_rows = rows_dev // stem_size
    inverse = jnp.zeros_like(index_order).at[index_order].set(jnp.arange(width, dtype=jnp.int32))
    reordered = jnp.take(branch_second, inverse, axis=1)
    powers = 2 ** jnp.arange(edge_values.shape[1], dtype=jnp.int32)
    codes = jnp.arange(edge_table.shape[0], dtype=jnp.int32)
    first = complex_dot(stem[0], branch_first).astype(jnp.bfloat16)
    low_half = first[:, :, :half_width]
    high_half = first[:, :, half_width:]
    outgoing = jnp.where(is_low, high_half, low_half)
    incoming = swapped(outgoing, "stem", bit_pos)
    joined = jnp.where(
        is_low,
        jnp.concatenate([low_half, incoming], axis=2),
        jnp.concatenate([incoming, high_half], axis=2),
    )
    second = complex_dot(joined, reordered).astype(jnp.bfloat16)
    contracted = complex_dot(second, branch_third)
    moved = lax.all_to_all(
        contracted.reshape(2, stem_size, block_rows, contracted.shape[2]),
        "stem",
        split_axis=1,
        concat_axis=1,
        tiled=True,
    )
    third = jnp.take(moved.reshape(2, rows_dev, contracted.shape[2]), picks, axis=1)
    code = jnp.sum(edge_values[0] * powers)
    onehot = (codes == code).astype(jnp.float32)
    factor = jnp.sum(onehot[:, None, None] * edge_table, axis=0)
    real = third[0] * factor[0][None, :] - third[1] * factor[1][None, :]
    imag = third[0] * factor[1][None, :] + third[1] * factor[0][None, :]
    total = jnp.stack([real, imag])
    return lax.psum(total, "cuts")


def solution(mesh):
    return jax.shard_map(
        on_device,
        mesh=mesh,
        in_specs=(
            P(("groups", "cuts"), None, "stem", None),
            P(("groups", "cuts"), None),
            P(),
            P(),
            P(),
            P(),
            P(),
            P("stem"),
        ),
        out_specs=P(None, ("groups", "stem"), None),
        check_vma=False,
    )
```

profile of v0, /device:TPU:11, one launch (start us, length us, event | category | flops | bytes accessed | tf_op | source)
XLA Modules:
  0.0 143.4 jit_solution(4913342444032320021)
XLA Ops:
  6.5 4.6 %fusion.2 = f32[512,1024]{1,0:T(8,128)} fusion(bf16[2,1024,1024]{2,1,0:T(8,128)(2,1)} %param.11, bf16[1,2,512,1024]{3,2,1,0:T(8,128)(2,1)} %param.8), kind=kOutput, calls=%fused_computation.11 | convolution fusion | flops 1073741824 | bytes 5242880 | tf_op jit(solution)/shard_map/dot_general | solution.py:14
  11.2 2.6 %fusion = f32[512,1024]{1,0:T(8,128)} fusion(bf16[2,1024,1024]{2,1,0:T(8,128)(2,1)S(1)} %copy-done.4, bf16[1,2,512,1024]{3,2,1,0:T(8,128)(2,1)S(1)} %copy-done.6), kind=kOutput, calls=%fused_computation.9 | convolution fusion | flops 1073741824 | bytes 5242880 | tf_op jit(solution)/shard_map/dot_general | solution.py:17
  13.8 3.6 %fusion.20 = bf16[1,512,1024]{2,1,0:T(8,128)(2,1)S(1)} fusion(f32[512,1024]{1,0:T(8,128)} %fusion.2, bf16[2,1024,1024]{2,1,0:T(8,128)(2,1)} %param.11, bf16[1,2,512,1024]{3,2,1,0:T(8,128)(2,1)S(1)} %copy-done.6), kind=kOutput, calls=%fused_computation.29 | convolution fusion | flops 1074790400 | bytes 6291456 | tf_op jit(solution)/shard_map/dot_general | solution.py:14
  17.9 1.3 fusion.23
  19.7 2.4 %collective-permute-start = (bf16[2,512,512]{2,1,0:T(8,128)(2,1)S(1)}, bf16[2,512,512]{2,1,0:T(8,128)(2,1)}, u32[]{:S(2)}, u32[]{:S(2)}) collective-permute-start(bf16[2,512,512]{2,1,0:T(8,128)(2,1)S(1)} %get-tuple-element.5), channel_id=1, source_target_pairs={{0,8},{2,10},{4,12},{6,14},{8,0},{10,2},{12,4},{14,6},{1,9},{3,11}... | collective-permute-start | bytes 3145736 | tf_op jit(solution)/shard_map/ppermute | solution.py:10
  22.1 4.5 %scatter_custom_fusion = s32[1024]{0:T(1024)S(1)} fusion(s32[1024]{0:T(1024)S(1)} %compare_select_fusion.1, s32[1024]{0:T(1024)S(1)} %iota.11, s32[]{:T(128)} %constant.69.clone.1), kind=kCustom, calls=%fused_computation.69 | custom fusion | bytes 4100 | tf_op jit(solution)/shard_map/scatter | solution.py:34
  26.6 27.6 %gather_fusion = bf16[1024,2,1024]{2,0,1:T(8,128)(2,1)} fusion(bf16[2,1024,1024]{2,1,0:T(8,128)(2,1)} %param.12, s32[1024]{0:T(1024)S(1)} %fusion.46), kind=kCustom, calls=%fused_computation | custom fusion | bytes 8392704 | tf_op jit(solution)/shard_map/jit(_take)/gather | solution.py:35
  54.2 2.6 %select_bitcast_fusion = bf16[2,1024,1024]{2,1,0:T(8,128)(2,1)S(1)} fusion(bf16[1024,2,1024]{2,0,1:T(8,128)(2,1)} %gather_fusion, pred[1024]{0:T(1024)(128)(4,1)S(1)} %compare_and_fusion), kind=kLoop, calls=%fused_computation.3 | loop fusion | flops 2097152 | bytes 8389632 | tf_op jit(solution)/shard_map/jit(_take)/select_n | solution.py:35
  56.9 10.4 %collective-permute-done = bf16[2,512,512]{2,1,0:T(8,128)(2,1)} collective-permute-done((bf16[2,512,512]{2,1,0:T(8,128)(2,1)S(1)}, bf16[2,512,512]{2,1,0:T(8,128)(2,1)}, u32[]{:S(2)}, u32[]{:S(2)}) %collective-permute-start) | collective-permute-done | bytes 1048608 | tf_op jit(solution)/shard_map/ppermute | solution.py:10
  67.3 2.2 %maximum_select_fusion = bf16[2,512,1024]{2,1,0:T(8,128)(2,1)S(1)} fusion(bf16[2,512,512]{2,1,0:T(8,128)(2,1)} %collective-permute-done, bf16[2,512,512]{2,1,0:T(8,128)(2,1)S(1)} %get-tuple-element.6, bf16[2,512,512]{2,1,0:T(8,128)(2,1)S(1)} %get-tuple-element.7, pred[]{:T(512)S(6)} %eq.15), kind=kLoop, calls=%fused_computation.8 | loop fusion | flops 9437184 | bytes 5242881 | tf_op jit(solution)/shard_map/jit(_where)/select_n | solution.py:43
  69.5 1.3 fusion.8
  70.8 1.3 fusion.11
  72.1 1.3 subtract_convert_fusion
  74.3 1.3 add_convert_fusion
  76.6 1.1 pad_maximum_fusion.1
  77.6 6.6 %all-to-all-start = ((f32[2,8,64,256]{3,2,0,1:T(8,128)}), f32[2,8,64,256]{3,2,0,1:T(8,128)S(1)}, u32[]{:S(2)}, u32[]{:S(2)}) async-start(f32[2,8,64,256]{3,2,0,1:T(8,128)} %pad_maximum_fusion.1), calls=%async_computation | async-start | bytes 2097152 | tf_op jit(solution)/shard_map/all_to_all | solution.py:50
  84.3 0.6 fusion.52
  84.9 0.6 compare_convert_fusion
  85.6 21.9 %all-to-all-done = f32[2,8,64,256]{3,2,0,1:T(8,128)S(1)} async-done(((f32[2,8,64,256]{3,2,0,1:T(8,128)}), f32[2,8,64,256]{3,2,0,1:T(8,128)S(1)}, u32[]{:S(2)}, u32[]{:S(2)}) %all-to-all-start) | async-done | bytes 1048608 | tf_op jit(solution)/shard_map/all_to_all | solution.py:50
  107.6 0.8 copy.17
  108.4 2.6 %gather_fusion.1 = f32[512,2,256]{2,1,0:T(2,128)S(1)} fusion(f32[2,512,256]{2,0,1:T(2,128)S(1)} %bitcast.83, s32[1024]{0:T(1024)S(1)} %pad_clamp_fusion), kind=kCustom, calls=%fused_computation.1 | custom fusion | bytes 2099200 | tf_op jit(solution)/shard_map/jit(_take)/gather | solution.py:57
  111.2 1.0 pad_maximum_fusion.2
  112.3 22.0 %all-reduce.2.cloned.1.call-done = f32[2,512,256]{2,1,0:T(8,128)} async-done(((f32[2,512,256]{2,1,0:T(8,128)}), f32[2,512,256]{2,1,0:T(8,128)}) %all-reduce.2.cloned.1.call-update) | async-done | bytes 1048592 | tf_op jit(solution)/shard_map/psum | solution.py:64
  134.3 2.3 %copy.23 = f32[2,512,256]{2,1,0:T(8,128)} copy(f32[2,512,256]{2,1,0:T(8,128)} %all-reduce.2.cloned.1.call-done) | data formatting | bytes 2097152
  (36 shorter events, 3.2 us)
Async XLA Ops:
  6.5 4.6 %copy-start.4 = (bf16[2,1024,1024]{2,1,0:T(8,128)(2,1)S(1)}, bf16[2,1024,1024]{2,1,0:T(8,128)(2,1)}, u32[]{:S(2)}) copy-start(bf16[2,1024,1024]{2,1,0:T(8,128)(2,1)} %param.11) | copy-start | bytes 12582916
  6.5 4.6 %copy-start.6 = (bf16[1,2,512,1024]{3,2,1,0:T(8,128)(2,1)S(1)}, bf16[1,2,512,1024]{3,2,1,0:T(8,128)(2,1)}, u32[]{:S(2)}) copy-start(bf16[1,2,512,1024]{3,2,1,0:T(8,128)(2,1)} %param.8) | copy-start | bytes 6291460
  13.8 3.6 %copy-start.5 = (bf16[2,1024,1024]{2,1,0:T(8,128)(2,1)S(1)}, bf16[2,1024,1024]{2,1,0:T(8,128)(2,1)}, u32[]{:S(2)}) copy-start(bf16[2,1024,1024]{2,1,0:T(8,128)(2,1)} %param.11) | copy-start | bytes 12582916
  13.8 4.1 %copy-start.8 = (f32[512,1024]{1,0:T(8,128)S(1)}, f32[512,1024]{1,0:T(8,128)}, u32[]{:S(2)}) copy-start(f32[512,1024]{1,0:T(8,128)} %fusion) | copy-start | bytes 6291460
  19.2 2.9 %copy-start.3 = (s32[1024]{0:T(1024)S(1)}, s32[1024]{0:T(1024)}, u32[]{:S(2)}) copy-start(s32[1024]{0:T(1024)} %param.10) | copy-start | bytes 12292
  19.7 47.6 %collective-permute-start = (bf16[2,512,512]{2,1,0:T(8,128)(2,1)S(1)}, bf16[2,512,512]{2,1,0:T(8,128)(2,1)}, u32[]{:S(2)}, u32[]{:S(2)}) collective-permute-start(bf16[2,512,512]{2,1,0:T(8,128)(2,1)S(1)} %get-tuple-element.5), channel_id=1, source_target_pairs={{0,8},{2,10},{4,12},{6,14},{8,0},{10,2},{12,4},{14,6},{1,9},{3,11}... | collective-permute-start | bytes 3145736 | tf_op jit(solution)/shard_map/ppermute | solution.py:10
  72.1 1.3 copy-start
  76.5 7.7 %copy-start.7 = (s32[1,4]{1,0:T(1,128)S(1)}, s32[1,4]{1,0:T(1,128)}, u32[]{:S(2)}) copy-start(s32[1,4]{1,0:T(1,128)} %param.9) | copy-start | bytes 52
  76.5 8.9 %copy-start.2 = (s32[512]{0:T(512)S(1)}, s32[512]{0:T(512)}, u32[]{:S(2)}) copy-start(s32[512]{0:T(512)} %param.15) | copy-start | bytes 6148
  76.6 8.9 %copy-start.1 = (f32[16,2,256]{2,1,0:T(2,128)S(1)}, f32[16,2,256]{2,1,0:T(2,128)}, u32[]{:S(2)}) copy-start(f32[16,2,256]{2,1,0:T(2,128)} %param.14) | copy-start | bytes 98308
  77.6 29.9 %all-to-all-start = ((f32[2,8,64,256]{3,2,0,1:T(8,128)}), f32[2,8,64,256]{3,2,0,1:T(8,128)S(1)}, u32[]{:S(2)}, u32[]{:S(2)}) async-start(f32[2,8,64,256]{3,2,0,1:T(8,128)} %pad_maximum_fusion.1), calls=%async_computation | async-start | bytes 2097152 | tf_op jit(solution)/shard_map/all_to_all | solution.py:50
  84.2 50.0 %all-reduce.2.cloned.1.call-start = ((), (), s32[]{:S(2)}) async-start(), calls=%async_computation.1 | async-start | bytes 2097152 | tf_op jit(solution)/shard_map/psum | solution.py:64
Sparse Core Ops, SparseCore 0:
  112.4 21.8 all-reduce.1
where the time goes:
time: 145 us; the launch traced here: 143 us
  waiting for transfers between devices  54.4 us (38%)
  local copies, waits for them, and re-layouts  38.3 us (26%)
  matrix products  19.1 us (13%)
  between operations  13.6 us (9%)
  other arithmetic  9.01 us (6%)
  starting transfers between devices  8.99 us (6%)
    gather x1, local copies, waits for them, and re-layouts, on_device(): reordered = jnp.take(branch_second, inverse, axis=1)  27.6 us
    psum x1, waiting for transfers between devices, on_device(): return lax.psum(total, 'cuts')  22 us
    all_to_all x1, waiting for transfers between devices, on_device(): lax.all_to_all(contracted.reshape(2, stem_size, block_rows, contracted.sh...  21.9 us
    ppermute x1, waiting for transfers between devices, swapped(): return lax.ppermute(value, axis, pairs)  10.4 us
    all_to_all x1, starting transfers between devices, on_device(): lax.all_to_all(contracted.reshape(2, stem_size, block_rows, contracted.sh...  6.61 us
    dot_general x3, matrix products, complex_dot(): jnp.dot(operand[1], matrix[1], preferred_element_type=jnp.float32)  6.33 us
    dot_general x3, matrix products, complex_dot(): jnp.dot(operand[0], matrix[0], preferred_element_type=jnp.float32)  5.36 us
    scatter x1, local copies, waits for them, and re-layouts, on_device(): jnp.zeros_like(index_order).at[index_order]  4.49 us
  transfers between devices with their start and end apart: 3, of which 3 were waited for; matrix products, arithmetic and copies ran while one was open for 25% of the time, Pallas kernels for 0%

commit v1 on v0

v1 whole, which is shorter than its diff:
```python
import functools

import jax
import jax.numpy as jnp
from jax import lax
from jax.experimental import pallas as pl
from jax.experimental.pallas import tpu as pltpu
from jax.sharding import PartitionSpec as P

MESH = pl.DeviceIdType.MESH
CHUNKS = 4


def dot(a, b):
    return jnp.dot(a, b, preferred_element_type=jnp.float32)


def contract_kernel(
    n, edges_ref, order_ref, table_ref, stem_hbm, first_hbm, second_hbm, third_hbm, out_hbm,
    stem, b1, b2, b3, pick, joint, gathered, firsts, partial, other, slab,
    load_sem, own_sem, pass_send, pass_recv, send_sem, recv_sem, copy_send, copy_recv,
):
    me = lax.axis_index("stem")
    core = lax.axis_index("cuts")
    mate = 1 - core
    half = n // 2
    top = me // half
    _, rows, width = stem.shape
    open_width = table_ref.shape[2]
    part = open_width // 2
    half_width = width // 2
    chunk = rows // CHUNKS
    block = rows // n
    owners = chunk // block

    loads = [
        pltpu.make_async_copy(second_hbm.at[0], b2.at[0], load_sem.at[0]),
        pltpu.make_async_copy(second_hbm.at[1], b2.at[1], load_sem.at[1]),
        pltpu.make_async_copy(third_hbm.at[0], b3.at[:, pl.ds(0, open_width)], load_sem.at[2]),
        pltpu.make_async_copy(third_hbm.at[1], b3.at[:, pl.ds(open_width, open_width)], load_sem.at[3]),
        pltpu.make_async_copy(first_hbm, b1, load_sem.at[4]),
        pltpu.make_async_copy(stem_hbm, stem, load_sem.at[5]),
    ]
    for load in loads:
        load.start()

    barrier = pltpu.get_barrier_semaphore()
    pl.semaphore_signal(barrier, inc=1, device_id={"cuts": mate}, device_id_type=MESH)

    @pl.loop(1, n)
    def _(step):
        pl.semaphore_signal(barrier, inc=1, device_id={"stem": (me + step) % n}, device_id_type=MESH)

    code = edges_ref[0, 0]
    for edge in range(1, edges_ref.shape[1]):
        code = code + edges_ref[0, edge] * 2**edge
    factor = table_ref[code]
    factor_re, factor_im = factor[0:1], factor[1:2]

    tile = half_width // 4
    for at in range(4):
        wanted = lax.broadcasted_iota(jnp.int32, (tile, width), 0) + (top * half_width + at * tile)
        hit = (order_ref[...] == wanted).astype(jnp.float32).astype(jnp.bfloat16)
        pick[at * tile : (at + 1) * tile, :] = hit

    for load in loads[:4]:
        load.wait()
    tall = width // 4

    @pl.loop(0, 4)
    def _(at):
        here = pl.ds(pl.multiple_of(at * tall, tall), tall)
        by_re = dot(b2[0, here, :], b3[...])
        by_im = dot(b2[1, here, :], b3[...])
        real = by_re[:, :open_width] - by_im[:, open_width:]
        imag = by_re[:, open_width:] + by_im[:, :open_width]
        joint[here, :open_width] = (real * factor_re - imag * factor_im).astype(jnp.bfloat16)
        joint[here, open_width:] = (real * factor_im + imag * factor_re).astype(jnp.bfloat16)

    gathered[...] = dot(pick[...], joint[...]).astype(jnp.bfloat16)

    for load in loads[4:]:
        load.wait()
    pl.semaphore_wait(barrier, n)

    def start_of(index):
        return (index + (1 - top) * (CHUNKS // 2)) % CHUNKS

    def passing(index):
        return pltpu.make_async_remote_copy(
            src_ref=partial.at[index, :, :, pl.ds(pl.multiple_of(mate * part, part), part)],
            dst_ref=other.at[index],
            send_sem=pass_send.at[index],
            recv_sem=pass_recv.at[index],
            device_id={"cuts": mate},
            device_id_type=MESH,
        )

    def sending(owner):
        return pltpu.make_async_remote_copy(
            src_ref=slab.at[owner],
            dst_ref=out_hbm.at[core, me],
            send_sem=send_sem.at[owner],
            recv_sem=recv_sem.at[me],
            device_id={"stem": owner},
            device_id_type=MESH,
        )

    def receiving(source):
        return pltpu.make_async_remote_copy(
            src_ref=slab.at[source],
            dst_ref=out_hbm.at[core, source],
            send_sem=send_sem.at[source],
            recv_sem=recv_sem.at[source],
            device_id={"stem": source},
            device_id_type=MESH,
        )

    def copying(source, src, column):
        return pltpu.make_async_remote_copy(
            src_ref=src,
            dst_ref=out_hbm.at[column, source],
            send_sem=copy_send.at[source],
            recv_sem=copy_recv.at[source],
            device_id={"cuts": mate},
            device_id_type=MESH,
        )

    @pl.loop(0, CHUNKS + 1)
    def _(index):
        @pl.when(index < CHUNKS)
        def _():
            here = pl.ds(pl.multiple_of(start_of(index) * chunk, chunk), chunk)
            step = open_width
            operand = stem[:, here, :].reshape(2 * chunk, width)
            for at in range(0, width, step):
                by_re = dot(operand, b1[0, :, at : at + step])
                by_im = dot(operand, b1[1, :, at : at + step])
                firsts[:chunk, at : at + step] = (by_re[:chunk] - by_im[chunk:]).astype(jnp.bfloat16)
                firsts[chunk:, at : at + step] = (by_im[:chunk] + by_re[chunk:]).astype(jnp.bfloat16)
            for t in range(2):
                got = dot(firsts[:, t * half_width : (t + 1) * half_width], gathered[...])
                partial[index, t] = got[:chunk, :open_width] - got[chunk:, open_width:]
                partial[index, 2 + t] = got[:chunk, open_width:] + got[chunk:, :open_width]
            passing(index).start()

        @pl.when(index > 0)
        def _():
            last = index - 1
            passing(last).wait_recv()
            mine = pl.ds(pl.multiple_of(core * part, part), part)
            total = partial[last, :, :, mine] + other[last]
            for at in range(owners):
                owner = start_of(last) * owners + at
                for c in range(2):
                    both = [total[2 * c + t, at * block : (at + 1) * block] for t in range(2)]
                    slab[owner, c] = jnp.concatenate(both, axis=0).astype(jnp.bfloat16)

                @pl.when(owner != me)
                def _():
                    sending(owner).start()

    own = pltpu.make_async_copy(slab.at[me], out_hbm.at[core, me], own_sem)
    own.start()
    copying(me, slab.at[me], core).start()

    @pl.loop(1, n)
    def _(step):
        source = (me + step) % half + ((top + step // half) % 2) * half
        receiving(source).wait_recv()
        copying(source, out_hbm.at[core, source], core).start()

    own.wait()

    @pl.loop(0, n)
    def _(source):
        copying(source, out_hbm.at[core, source], mate).wait()

        @pl.when(source != me)
        def _():
            receiving(source).wait_send()

    @pl.loop(0, CHUNKS)
    def _(index):
        passing(index).wait_send()


def pick_kernel(n, picks_ref, parts_ref, out_ref):
    half = n // 2
    rows = out_ref.shape[1]
    block = rows // n
    part = parts_ref.shape[4]
    at = lax.broadcasted_iota(jnp.int32, (rows, rows), 0)
    u, rest = at // (2 * block), at % (2 * block)
    row = (rest // block) * (half * block) + u * block + rest % block
    hit = (picks_ref[...] == row).astype(jnp.float32).astype(jnp.bfloat16)
    for c in range(2):
        total = None
        for h in range(2):
            sides = [parts_ref[k, h * half : (h + 1) * half, c].reshape(rows, part) for k in range(2)]
            got = lax.dot_general(
                hit, jnp.concatenate(sides, axis=1), (((0,), (0,)), ((), ())), preferred_element_type=jnp.float32
            )
            total = got if total is None else total + got
        out_ref[c] = total


def solution(mesh):
    n = mesh.shape["stem"]

    def on_device(stem, edge_values, index_order, branch_first, branch_second, branch_third, edge_table, picks):
        _, _, rows, width = stem.shape
        open_width = branch_third.shape[2]
        part = open_width // 2
        block = rows // n
        chunk = rows // CHUNKS
        bf16, f32 = jnp.bfloat16, jnp.float32
        vmem = pl.BlockSpec(memory_space=pltpu.VMEM)
        anywhere = pl.BlockSpec(memory_space=pl.ANY)
        dma = pltpu.SemaphoreType.DMA
        parts = pl.pallas_call(
            functools.partial(contract_kernel, n),
            out_shape=jax.ShapeDtypeStruct((2, n, 2, 2 * block, part), bf16),
            in_specs=[pl.BlockSpec(memory_space=pltpu.SMEM), vmem, vmem] + [anywhere] * 4,
            out_specs=anywhere,
            scratch_shapes=[
                pltpu.VMEM((2, rows, width), bf16),
                pltpu.VMEM((2, width, width), bf16),
                pltpu.VMEM((2, width, width), bf16),
                pltpu.VMEM((width, 2 * open_width), bf16),
                pltpu.VMEM((width // 2, width), bf16),
                pltpu.VMEM((width, 2 * open_width), bf16),
                pltpu.VMEM((width // 2, 2 * open_width), bf16),
                pltpu.VMEM((2 * chunk, width), bf16),
                pltpu.VMEM((CHUNKS, 4, chunk, open_width), f32),
                pltpu.VMEM((CHUNKS, 4, chunk, part), f32),
                pltpu.VMEM((n, 2, 2 * block, part), bf16),
                dma((6,)),
                dma,
                dma((CHUNKS,)),
                dma((CHUNKS,)),
                dma((n,)),
                dma((n,)),
                dma((n,)),
                dma((n,)),
            ],
            compiler_params=pltpu.CompilerParams(
                collective_id=0, has_side_effects=True, vmem_limit_bytes=48 * 2**20
            ),
            cost_estimate=pl.CostEstimate(flops=8 * 10**9, bytes_accessed=13 * 2**20, transcendentals=0),
        )(
            edge_values, index_order.reshape(1, width), edge_table,
            stem[0], branch_first, branch_second, branch_third,
        )
        return pl.pallas_call(
            functools.partial(pick_kernel, n),
            out_shape=jax.ShapeDtypeStruct((2, picks.shape[0], open_width), f32),
            in_specs=[vmem, vmem],
            out_specs=vmem,
            compiler_params=pltpu.CompilerParams(vmem_limit_bytes=32 * 2**20),
        )(picks.reshape(1, picks.shape[0]), parts)

    return jax.shard_map(
        on_device,
        mesh=mesh,
        in_specs=(
            P(("groups", "cuts"), None, "stem", None),
            P(("groups", "cuts"), None),
            P(),
            P(),
            P(),
            P(),
            P(),
            P("stem"),
        ),
        out_specs=P(None, ("groups", "stem"), None),
        check_vma=False,
    )
```

time: 145 us -> 32.3 us (0.22)
  waiting for transfers between devices: 54.4 us -> 0 us
  local copies, waits for them, and re-layouts: 38.3 us -> 4.92 us
  Pallas kernels: 0 us -> 27.1 us
  matrix products: 19.1 us -> 0 us
  between operations: 13.6 us -> 0.02 us
  other arithmetic: 9.01 us -> 0 us
  starting transfers between devices: 8.99 us -> 0 us
    gather x2 -> x0, local copies, waits for them, and re-layouts: 30.2 us -> none  [the longest x1 27.6 us: on_device(): reordered = jnp.take(branch_second, inverse, axis=1)]
    pallas_call x0 -> x2, Pallas kernels: none -> 27.1 us  [the longest x1 25.3 us: on_device(): pl.pallas_call(functools.partial(contract_kernel, n), out_shape=jax.Shape...]
    psum x1 -> x0, waiting for transfers between devices: 22 us -> none  [on_device(): return lax.psum(total, 'cuts')]
    all_to_all x1 -> x0, waiting for transfers between devices: 21.9 us -> none  [on_device(): lax.all_to_all(contracted.reshape(2, stem_size, block_rows, contracted.sh...]
    dot_general x12 -> x0, matrix products: 19.1 us -> none  [the longest x3 6.33 us: complex_dot(): jnp.dot(operand[1], matrix[1], preferred_element_type=jnp.float32)]
    ppermute x1 -> x0, waiting for transfers between devices: 10.4 us -> none  [swapped(): return lax.ppermute(value, axis, pairs)]
    all_to_all x1 -> x0, starting transfers between devices: 6.61 us -> none  [on_device(): lax.all_to_all(contracted.reshape(2, stem_size, block_rows, contracted.sh...]
    select_n x6 -> x0, other arithmetic: 5.48 us -> none  [the longest x1 2.63 us: on_device(): reordered = jnp.take(branch_second, inverse, axis=1)]
  transfers between devices with their start and end apart: 3 -> 0, of which waited for: 3 -> 0; matrix products, arithmetic and copies ran while one was open for 25% -> 0% of each run, Pallas kernels for 0% -> 0%
where the time goes in v1:
time: 32.3 us; the launch traced here: 32 us
  Pallas kernels  27.1 us (84%)
  local copies, waits for them, and re-layouts  4.92 us (15%)
    pallas_call x1, Pallas kernels, on_device(): pl.pallas_call(functools.partial(contract_kernel, n), out_shape=jax.Shape...  25.3 us
    unnamed x12, local copies, waits for them, and re-layouts  4.92 us
    pallas_call x1, Pallas kernels, on_device(): pl.pallas_call(functools.partial(pick_kernel, n), out_shape=jax.ShapeDtyp...  1.75 us

profile of v1, /device:TPU:11, one launch (start us, length us, event | category | flops | bytes accessed | tf_op | source)
XLA Modules:
  0.0 32.0 jit_solution(68908828584755548)
XLA Ops:
  0.0 0.0 copy-start.1
  0.0 1.6 %copy-done.1 = bf16[1,2,512,1024]{3,2,1,0:T(8,128)(2,1)S(1)} copy-done((bf16[1,2,512,1024]{3,2,1,0:T(8,128)(2,1)S(1)}, bf16[1,2,512,1024]{3,2,1,0:T(8,128)(2,1)}, u32[]{:S(2)}) %copy-start.1) | copy-done | bytes 2097176
  1.6 0.0 copy-start.2
  1.6 1.2 %copy-done.2 = bf16[2,1024,256]{2,1,0:T(8,128)(2,1)S(1)} copy-done((bf16[2,1024,256]{2,1,0:T(8,128)(2,1)S(1)}, bf16[2,1024,256]{2,1,0:T(8,128)(2,1)}, u32[]{:S(2)}) %copy-start.2) | copy-done | bytes 1048600
  2.8 0.0 copy-start.3
  2.8 0.8 %copy-done.3 = f32[16,2,256]{2,1,0:T(2,128)S(1)} copy-done((f32[16,2,256]{2,1,0:T(2,128)S(1)}, f32[16,2,256]{2,1,0:T(2,128)}, u32[]{:S(2)}) %copy-start.3) | copy-done | bytes 32792
  3.6 0.0 copy-start.4
  3.6 0.7 %copy-done.4 = s32[1024]{0:T(1024)S(1)} copy-done((s32[1024]{0:T(1024)S(1)}, s32[1024]{0:T(1024)}, u32[]{:S(2)}) %copy-start.4) | copy-done | bytes 4120
  4.3 0.0 copy-start.5
  4.3 0.7 %copy-done.5 = s32[1,4]{1,0:T(1,128)S(1)} copy-done((s32[1,4]{1,0:T(1,128)S(1)}, s32[1,4]{1,0:T(1,128)}, u32[]{:S(2)}) %copy-start.5) | copy-done | bytes 40
  4.9 0.0 copy-start
  4.9 25.3 %shard_map.82.parts_ref = bf16[2,8,2,128,128]{4,3,2,1,0:T(8,128)(2,1)S(1)} custom-call(s32[1,4]{1,0:T(1,128)S(1)} %copy-done.5, s32[1,1024]{1,0:T(1,128)S(1)} %bitcast.5, f32[16,2,256]{2,1,0:T(2,128)S(1)} %copy-done.3, bf16[2,512,1024]{2,1,0:T(8,128)(2,1)S(1)} %bitcast.4, bf16[2,1024,1024]{2,1,0:T(8,128)(2,1)} %first_hbm.1, ...), custom_call_target="tpu_custom_call" | custom-call | flops 8000000000 | bytes 13631488 | tf_op jit(solution)/shard_map/pallas_call | solution.py:221
  30.2 0.0 copy-done
  30.2 1.8 %shard_map.83 = f32[2,512,256]{2,1,0:T(8,128)} custom-call(s32[1,512]{1,0:T(1,128)S(1)} %bitcast.3, bf16[2,8,2,128,128]{4,3,2,1,0:T(8,128)(2,1)S(1)} %shard_map.82.parts_ref), custom_call_target="tpu_custom_call" | custom-call | tf_op jit(solution)/shard_map/pallas_call | solution.py:255
Async XLA Ops:
  0.0 1.6 %copy-start.1 = (bf16[1,2,512,1024]{3,2,1,0:T(8,128)(2,1)S(1)}, bf16[1,2,512,1024]{3,2,1,0:T(8,128)(2,1)}, u32[]{:S(2)}) copy-start(bf16[1,2,512,1024]{3,2,1,0:T(8,128)(2,1)} %param.8) | copy-start | bytes 6291460
  1.6 1.2 %copy-start.2 = (bf16[2,1024,256]{2,1,0:T(8,128)(2,1)S(1)}, bf16[2,1024,256]{2,1,0:T(8,128)(2,1)}, u32[]{:S(2)}) copy-start(bf16[2,1024,256]{2,1,0:T(8,128)(2,1)} %third_hbm.1) | copy-start | bytes 3145732
  2.8 0.8 %copy-start.3 = (f32[16,2,256]{2,1,0:T(2,128)S(1)}, f32[16,2,256]{2,1,0:T(2,128)}, u32[]{:S(2)}) copy-start(f32[16,2,256]{2,1,0:T(2,128)} %table_ref.1) | copy-start | bytes 98308
  3.6 0.7 %copy-start.4 = (s32[1024]{0:T(1024)S(1)}, s32[1024]{0:T(1024)}, u32[]{:S(2)}) copy-start(s32[1024]{0:T(1024)} %param.10) | copy-start | bytes 12292
  4.3 0.7 %copy-start.5 = (s32[1,4]{1,0:T(1,128)S(1)}, s32[1,4]{1,0:T(1,128)}, u32[]{:S(2)}) copy-start(s32[1,4]{1,0:T(1,128)} %edges_ref.1) | copy-start | bytes 52
  4.9 25.3 %copy-start = (s32[512]{0:T(512)S(1)}, s32[512]{0:T(512)}, u32[]{:S(2)}) copy-start(s32[512]{0:T(512)} %param.15) | copy-start | bytes 6148

commit v2 on v1

--- a/solution.py
+++ b/solution.py
@@ -8,7 +8,8 @@
 from jax.sharding import PartitionSpec as P
 
 MESH = pl.DeviceIdType.MESH
-CHUNKS = 4
+CHUNKS = 8
+TILES = 4
 
 
 def dot(a, b):
@@ -16,9 +17,9 @@
 
 
 def contract_kernel(
-    n, edges_ref, order_ref, table_ref, stem_hbm, first_hbm, second_hbm, third_hbm, out_hbm,
-    stem, b1, b2, b3, pick, joint, gathered, firsts, partial, other, slab,
-    load_sem, own_sem, pass_send, pass_recv, send_sem, recv_sem, copy_send, copy_recv,
+    n, edges_hbm, order_hbm, table_hbm, stem_hbm, first_hbm, second_hbm, third_hbm, out_hbm,
+    edges_ref, order_ref, table_ref, stem, b1, b2, b3, pick, joint, gathered, firsts, partial, other, slab,
+    load_sem, tile_sem, own_sem, pass_send, pass_recv, send_sem, recv_sem, copy_send, copy_recv,
 ):
     me = lax.axis_index("stem")
     core = lax.axis_index("cuts")
@@ -33,15 +34,25 @@
     block = rows // n
     owners = chunk // block
 
+    tall = width // TILES
     loads = [
-        pltpu.make_async_copy(second_hbm.at[0], b2.at[0], load_sem.at[0]),
-        pltpu.make_async_copy(second_hbm.at[1], b2.at[1], load_sem.at[1]),
-        pltpu.make_async_copy(third_hbm.at[0], b3.at[:, pl.ds(0, open_width)], load_sem.at[2]),
-        pltpu.make_async_copy(third_hbm.at[1], b3.at[:, pl.ds(open_width, open_width)], load_sem.at[3]),
-        pltpu.make_async_copy(first_hbm, b1, load_sem.at[4]),
+        pltpu.make_async_copy(third_hbm.at[0], b3.at[:, pl.ds(0, open_width)], load_sem.at[0]),
+        pltpu.make_async_copy(third_hbm.at[1], b3.at[:, pl.ds(open_width, open_width)], load_sem.at[1]),
+        pltpu.make_async_copy(order_hbm, order_ref, load_sem.at[2]),
+        pltpu.make_async_copy(table_hbm, table_ref, load_sem.at[3]),
+        pltpu.make_async_copy(edges_hbm, edges_ref, load_sem.at[4]),
+    ]
+    tiles = [
+        pltpu.make_async_copy(
+            second_hbm.at[:, pl.ds(at * tall, tall)], b2.at[:, pl.ds(at * tall, tall)], tile_sem.at[at]
+        )
+        for at in range(TILES)
+    ]
+    later = [
         pltpu.make_async_copy(stem_hbm, stem, load_sem.at[5]),
+        pltpu.make_async_copy(first_hbm, b1, load_sem.at[6]),
     ]
-    for load in loads:
+    for load in loads + tiles:
         load.start()
 
     barrier = pltpu.get_barrier_semaphore()
@@ -50,6 +61,14 @@
     @pl.loop(1, n)
     def _(step):
         pl.semaphore_signal(barrier, inc=1, device_id={"stem": (me + step) % n}, device_id_type=MESH)
+
+    for load in loads:
+        load.wait()
+    wide = half_width // TILES
+    for at in range(TILES):
+        wanted = lax.broadcasted_iota(jnp.int32, (wide, width), 0) + (top * half_width + at * wide)
+        hit = (order_ref[...] == wanted).astype(jnp.float32).astype(jnp.bfloat16)
+        pick[at * wide : (at + 1) * wide, :] = hit
 
     code = edges_ref[0, 0]
     for edge in range(1, edges_ref.shape[1]):
@@ -57,19 +76,12 @@
     factor = table_ref[code]
     factor_re, factor_im = factor[0:1], factor[1:2]
 
-    tile = half_width // 4
-    for at in range(4):
-        wanted = lax.broadcasted_iota(jnp.int32, (tile, width), 0) + (top * half_width + at * tile)
-        hit = (order_ref[...] == wanted).astype(jnp.float32).astype(jnp.bfloat16)
-        pick[at * tile : (at + 1) * tile, :] = hit
-
-    for load in loads[:4]:
-        load.wait()
-    tall = width // 4
-
-    @pl.loop(0, 4)
-    def _(at):
-        here = pl.ds(pl.multiple_of(at * tall, tall), tall)
+    for at in range(TILES):
+        tiles[at].wait()
+        if at == 0:
+            for load in later:
+                load.start()
+        here = slice(at * tall, (at + 1) * tall)
         by_re = dot(b2[0, here, :], b3[...])
         by_im = dot(b2[1, here, :], b3[...])
         real = by_re[:, :open_width] - by_im[:, open_width:]
@@ -79,9 +91,8 @@
 
     gathered[...] = dot(pick[...], joint[...]).astype(jnp.bfloat16)
 
-    for load in loads[4:]:
+    for load in later:
         load.wait()
-    pl.semaphore_wait(barrier, n)
 
     def start_of(index):
         return (index + (1 - top) * (CHUNKS // 2)) % CHUNKS
@@ -126,39 +137,45 @@
             device_id_type=MESH,
         )
 
-    @pl.loop(0, CHUNKS + 1)
+    def compute(index):
+        here = pl.ds(pl.multiple_of(start_of(index) * chunk, chunk), chunk)
+        step = open_width
+        operand = stem[:, here, :].reshape(2 * chunk, width)
+        for at in range(0, width, step):
+            by_re = dot(operand, b1[0, :, at : at + step])
+            by_im = dot(operand, b1[1, :, at : at + step])
+            firsts[:chunk, at : at + step] = (by_re[:chunk] - by_im[chunk:]).astype(jnp.bfloat16)
+            firsts[chunk:, at : at + step] = (by_im[:chunk] + by_re[chunk:]).astype(jnp.bfloat16)
+        for t in range(2):
+            got = dot(firsts[:, t * half_width : (t + 1) * half_width], gathered[...])
+            partial[index, t] = got[:chunk, :open_width] - got[chunk:, open_width:]
+            partial[index, 2 + t] = got[:chunk, open_width:] + got[chunk:, :open_width]
+
+    def finish(last):
+        passing(last).wait_recv()
+        mine = pl.ds(pl.multiple_of(core * part, part), part)
+        total = partial[last, :, :, mine] + other[last]
+        for at in range(owners):
+            owner = start_of(last) * owners + at
+            for c in range(2):
+                both = [total[2 * c + t, at * block : (at + 1) * block] for t in range(2)]
+                slab[owner, c] = jnp.concatenate(both, axis=0).astype(jnp.bfloat16)
+
+            @pl.when(owner != me)
+            def _():
+                sending(owner).start()
+
+    compute(0)
+    pl.semaphore_wait(barrier, n)
+    passing(0).start()
+
+    @pl.loop(1, CHUNKS)
     def _(index):
-        @pl.when(index < CHUNKS)
-        def _():
-            here = pl.ds(pl.multiple_of(start_of(index) * chunk, chunk), chunk)
-            step = open_width
-            operand = stem[:, here, :].reshape(2 * chunk, width)
-            for at in range(0, width, step):
-                by_re = dot(operand, b1[0, :, at : at + step])
-                by_im = dot(operand, b1[1, :, at : at + step])
-                firsts[:chunk, at : at + step] = (by_re[:chunk] - by_im[chunk:]).astype(jnp.bfloat16)
-                firsts[chunk:, at : at + step] = (by_im[:chunk] + by_re[chunk:]).astype(jnp.bfloat16)
-            for t in range(2):
-                got = dot(firsts[:, t * half_width : (t + 1) * half_width], gathered[...])
-                partial[index, t] = got[:chunk, :open_width] - got[chunk:, open_width:]
-                partial[index, 2 + t] = got[:chunk, open_width:] + got[chunk:, :open_width]
-            passing(index).start()
-
-        @pl.when(index > 0)
-        def _():
-            last = index - 1
-            passing(last).wait_recv()
-            mine = pl.ds(pl.multiple_of(core * part, part), part)
-            total = partial[last, :, :, mine] + other[last]
-            for at in range(owners):
-                owner = start_of(last) * owners + at
-                for c in range(2):
-                    both = [total[2 * c + t, at * block : (at + 1) * block] for t in range(2)]
-                    slab[owner, c] = jnp.concatenate(both, axis=0).astype(jnp.bfloat16)
-
-                @pl.when(owner != me)
-                def _():
-                    sending(owner).start()
+        compute(index)
+        passing(index).start()
+        finish(index - 1)
+
+    finish(CHUNKS - 1)
 
     own = pltpu.make_async_copy(slab.at[me], out_hbm.at[core, me], own_sem)
     own.start()
@@ -221,9 +238,12 @@
         parts = pl.pallas_call(
             functools.partial(contract_kernel, n),
             out_shape=jax.ShapeDtypeStruct((2, n, 2, 2 * block, part), bf16),
-            in_specs=[pl.BlockSpec(memory_space=pltpu.SMEM), vmem, vmem] + [anywhere] * 4,
+            in_specs=[pl.BlockSpec(memory_space=pltpu.HBM)] * 7,
             out_specs=anywhere,
             scratch_shapes=[
+                pltpu.SMEM(edge_values.shape, edge_values.dtype),
+                pltpu.VMEM((1, width), index_order.dtype),
+                pltpu.VMEM(edge_table.shape, edge_table.dtype),
                 pltpu.VMEM((2, rows, width), bf16),
                 pltpu.VMEM((2, width, width), bf16),
                 pltpu.VMEM((2, width, width), bf16),
@@ -235,7 +255,8 @@
                 pltpu.VMEM((CHUNKS, 4, chunk, open_width), f32),
                 pltpu.VMEM((CHUNKS, 4, chunk, part), f32),
                 pltpu.VMEM((n, 2, 2 * block, part), bf16),
-                dma((6,)),
+                dma((7,)),
+                dma((TILES,)),
                 dma,
                 dma((CHUNKS,)),
                 dma((CHUNKS,)),
@@ -245,7 +266,7 @@
                 dma((n,)),
             ],
             compiler_params=pltpu.CompilerParams(
-                collective_id=0, has_side_effects=True, vmem_limit_bytes=48 * 2**20
+                collective_id=0, has_side_effects=True, vmem_limit_bytes=62 * 2**20
             ),
             cost_estimate=pl.CostEstimate(flops=8 * 10**9, bytes_accessed=13 * 2**20, transcendentals=0),
         )(
@@ -257,7 +278,7 @@
             out_shape=jax.ShapeDtypeStruct((2, picks.shape[0], open_width), f32),
             in_specs=[vmem, vmem],
             out_specs=vmem,
-            compiler_params=pltpu.CompilerParams(vmem_limit_bytes=32 * 2**20),
+            compiler_params=pltpu.CompilerParams(vmem_limit_bytes=62 * 2**20),
         )(picks.reshape(1, picks.shape[0]), parts)
 
     return jax.shard_map(

time: 32.3 us -> 27.1 us (0.84)
  local copies, waits for them, and re-layouts: 4.92 us -> 0 us
  Pallas kernels: 27.1 us -> 26.7 us
    unnamed x12 -> x0, local copies, waits for them, and re-layouts: 4.92 us -> none
    pallas_call x1, Pallas kernels: 25.3 us -> 23.7 us  [on_device(): pl.pallas_call(functools.partial(contract_kernel, n), out_shape=jax.Shape...]
    pallas_call x1, Pallas kernels: 1.75 us -> 3 us  [on_device(): pl.pallas_call(functools.partial(pick_kernel, n), out_shape=jax.ShapeDtyp...]
where the time goes in v2:
time: 27.1 us; the launch traced here: 26.7 us
  Pallas kernels  26.7 us (99%)
    pallas_call x1, Pallas kernels, on_device(): pl.pallas_call(functools.partial(contract_kernel, n), out_shape=jax.Shape...  23.7 us
    pallas_call x1, Pallas kernels, on_device(): pl.pallas_call(functools.partial(pick_kernel, n), out_shape=jax.ShapeDtyp...  3 us

profile of v2, /device:TPU:11, one launch (start us, length us, event | category | flops | bytes accessed | tf_op | source)
XLA Modules:
  0.0 26.7 jit_solution(16733346762351205415)
XLA Ops:
  0.0 23.7 %shard_map.82.parts_ref = bf16[2,8,2,128,128]{4,3,2,1,0:T(8,128)(2,1)} custom-call(s32[1,4]{1,0:T(1,128)} %edges_hbm.1, s32[1,1024]{1,0:T(1,128)} %bitcast.5, f32[16,2,256]{2,1,0:T(2,128)} %table_hbm.1, bf16[2,512,1024]{2,1,0:T(8,128)(2,1)} %bitcast.4, bf16[2,1024,1024]{2,1,0:T(8,128)(2,1)} %first_hbm.1, bf16[2,1024,1024]{2,1,0:T(8,128)(2,1)} %second_hbm.1, ...), custom_call_target="tpu_custom_call" | custom-call | flops 8000000000 | bytes 13631488 | tf_op jit(solution)/shard_map/pallas_call | solution.py:238
  23.7 3.0 %shard_map.83 = f32[2,512,256]{2,1,0:T(8,128)} custom-call(s32[1,512]{1,0:T(1,128)} %bitcast.3, bf16[2,8,2,128,128]{4,3,2,1,0:T(8,128)(2,1)} %shard_map.82.parts_ref), custom_call_target="tpu_custom_call" | custom-call | tf_op jit(solution)/shard_map/pallas_call | solution.py:276

commit v3 on v2

--- a/solution.py
+++ b/solution.py
@@ -95,7 +95,10 @@
         load.wait()
 
     def start_of(index):
-        return (index + (1 - top) * (CHUNKS // 2)) % CHUNKS
+        side = (1 - top + index // (CHUNKS // 2)) % 2
+        count = CHUNKS // 2
+        at = index % count
+        return side * count + (at + (1 - me % 2) * (1 - 2 * (at % 2)))
 
     def passing(index):
         return pltpu.make_async_remote_copy(

time: 27.1 us -> 27.1 us (level)
  no operation moved by 1% of the time
where the time goes in v3:
time: 27.1 us; the launch traced here: 26.9 us
  Pallas kernels  26.9 us (99%)
    pallas_call x1, Pallas kernels, on_device(): pl.pallas_call(functools.partial(contract_kernel, n), out_shape=jax.Shape...  23.9 us
    pallas_call x1, Pallas kernels, on_device(): pl.pallas_call(functools.partial(pick_kernel, n), out_shape=jax.ShapeDtyp...  3 us

profile of v3, /device:TPU:11, one launch (start us, length us, event | category | flops | bytes accessed | tf_op | source)
XLA Modules:
  0.0 26.9 jit_solution(2714047027913974420)
XLA Ops:
  0.0 23.9 %shard_map.82.parts_ref = bf16[2,8,2,128,128]{4,3,2,1,0:T(8,128)(2,1)} custom-call(s32[1,4]{1,0:T(1,128)} %edges_hbm.1, s32[1,1024]{1,0:T(1,128)} %bitcast.5, f32[16,2,256]{2,1,0:T(2,128)} %table_hbm.1, bf16[2,512,1024]{2,1,0:T(8,128)(2,1)} %bitcast.4, bf16[2,1024,1024]{2,1,0:T(8,128)(2,1)} %first_hbm.1, bf16[2,1024,1024]{2,1,0:T(8,128)(2,1)} %second_hbm.1, ...), custom_call_target="tpu_custom_call" | custom-call | flops 8000000000 | bytes 13631488 | tf_op jit(solution)/shard_map/pallas_call | solution.py:241
  23.9 3.0 %shard_map.83 = f32[2,512,256]{2,1,0:T(8,128)} custom-call(s32[1,512]{1,0:T(1,128)} %bitcast.3, bf16[2,8,2,128,128]{4,3,2,1,0:T(8,128)(2,1)} %shard_map.82.parts_ref), custom_call_target="tpu_custom_call" | custom-call | tf_op jit(solution)/shard_map/pallas_call | solution.py:279
